TPU v7x, 32 devices: a whole 2x2x4 slice. The times are simulated.
32 devices in a mesh: run: 2 (over x), gy: 16 (over z, y, core).
Axes of the slice: x: 2, y: 2, z: 4, core: 2. Of those that a mesh axis runs over, the one named last changes fastest.
Arguments:
- conserved: float32 [5, 16, 128, 128], P(None, 'run', 'gy'), parts along dimension 1, may hold values from -1.5 to 5, as said below
- target: float32 [3, 16, 128, 128], P(None, 'run', 'gy'), parts along dimension 1, may hold values from -2 to 2
Outputs:
- grad_state: float32 [5, 16, 128, 128], P(None, 'run', 'gy'), parts along dimension 1
- vorticity: float32 [3, 16, 128, 128], P(None, 'run', 'gy'), parts along dimension 1
There are 2 independent parts, one for each index of `run`. A program takes and returns all parts, laid end to end along the dimension named above; each array names one. Nothing has to cross between parts.
Inputs may be any that keep to these rules, and one draw needn't show every extreme that they name: conserved[0] is the density, between 0.75 and 1.25; conserved[1:4] is density times a velocity of magnitude under 0.8 per component; conserved[4] is the total energy, with a pressure between 0.75 and 1.25.
All inputs are finite; a program needn't handle non-finite values.
Results may differ from a plain program's by a relative error of at most 0.00002.
Values sent between devices are 32-bit elements; how exact they have to be, the bound alone decides.
A program may use at most 64 MiB of HBM per device.

v0:
```python
import jax
import jax.numpy as jnp
from jax import lax
from jax.sharding import PartitionSpec as P

GAMMA = 1.4
SPEED = 2.5
DT = 0.2
weno_eps = 0.1


def padded_2(array, sides, width):
    for axis, dim in sides:
        count, length = (lax.axis_size(axis), array.shape[dim])
        up = [(i, (i + 1) % count) for i in range(count)]
        down = [(j, i) for i, j in up]
        last = lax.slice_in_dim(array, length - width, length, axis=dim)
        first = lax.slice_in_dim(array, 0, width, axis=dim)
        before = lax.ppermute(last, axis, up)
        after = lax.ppermute(first, axis, down)
        array = jnp.concatenate([before, array, after], axis=dim)
    return array


def weno_face(far_left, near_left, centre, near_right, far_right):
    cand_low = (2.0 * far_left - 7.0 * near_left + 11.0 * centre) / 6.0
    cand_mid = (-near_left + 5.0 * centre + 2.0 * near_right) / 6.0
    cand_high = (2.0 * centre + 5.0 * near_right - far_right) / 6.0
    smooth_low = (
        13.0 / 12.0 * (far_left - 2.0 * near_left + centre) ** 2
        + 0.25 * (far_left - 4.0 * near_left + 3.0 * centre) ** 2
    )
    middle_smoothness_indicator = (
        13.0 / 12.0 * (near_left - 2.0 * centre + near_right) ** 2
        + 0.25 * (near_left - near_right) ** 2
    )
    smooth_high = (
        13.0 / 12.0 * (centre - 2.0 * near_right + far_right) ** 2
        + 0.25 * (3.0 * centre - 4.0 * near_right + far_right) ** 2
    )
    contrast = (smooth_low - smooth_high) ** 2
    weight_low = 0.1 * (1.0 + contrast / (smooth_low + weno_eps) ** 2)
    weight_mid = 0.6 * (1.0 + contrast / (middle_smoothness_indicator + weno_eps) ** 2)
    weight_high = 0.3 * (1.0 + contrast / (smooth_high + weno_eps) ** 2)
    return (weight_low * cand_low + weight_mid * cand_mid + weight_high * cand_high) / (
        weight_low + weight_mid + weight_high
    )


def split_fluxes(conserved, direction):
    density = conserved[0]
    momentum = conserved[1:4]
    energy = conserved[4]
    velocity = momentum / density
    pressure = (GAMMA - 1.0) * (energy - 0.5 * jnp.sum(momentum * velocity, axis=0))
    normal_speed = velocity[direction]
    pieces = [momentum[direction]]
    for component in range(3):
        product_term = momentum[component] * normal_speed
        if component == direction:
            product_term = product_term + pressure
        pieces.append(product_term)
    pieces.append((energy + pressure) * normal_speed)
    flux_rows = jnp.stack(pieces)
    return (0.5 * (flux_rows + SPEED * conserved), 0.5 * (flux_rows - SPEED * conserved))


def face_values(plus_part, negative_split_flux, offset):

    def single(members):
        upper_part, lower_part = members
        from_left = weno_face(
            offset(upper_part, -2),
            offset(upper_part, -1),
            offset(upper_part, 0),
            offset(upper_part, 1),
            offset(upper_part, 2),
        )
        from_right = weno_face(
            offset(lower_part, 3),
            offset(lower_part, 2),
            offset(lower_part, 1),
            offset(lower_part, 0),
            offset(lower_part, -1),
        )
        return from_left + from_right

    return lax.map(jax.checkpoint(single), (plus_part, negative_split_flux))


def periodic_term(conserved, direction):
    plus_part, negative_split_flux = split_fluxes(conserved, direction)

    def offset(values, shift_by):
        return jnp.roll(values, -shift_by, axis=direction)

    face_flux = face_values(plus_part, negative_split_flux, offset)
    return -(face_flux - jnp.roll(face_flux, 1, axis=direction + 1))


def sliced_term(padded):
    plus_part, negative_split_flux = split_fluxes(padded, 1)
    length = padded.shape[2]

    def offset(values, shift_by):
        return lax.slice_in_dim(values, 2 + shift_by, length - 3 + shift_by, axis=1)

    face_flux = face_values(plus_part, negative_split_flux, offset)
    return -(face_flux[:, :, 1:] - face_flux[:, :, :-1])


def rate_padded(padded):
    interior = padded[:, :, 3:-3]
    return periodic_term(interior, 0) + sliced_term(padded) + periodic_term(interior, 2)


def section_rate(padded):
    return jax.checkpoint(rate_padded)(padded)


def central(values, direction):
    return 0.5 * (jnp.roll(values, -1, axis=direction) - jnp.roll(values, 1, axis=direction))


def across_y(values):
    return 0.5 * (values[:, 2:] - values[:, :-2])


def curl_padded(velocity_pad):
    interior = velocity_pad[:, :, 1:-1]
    return jnp.stack(
        [
            across_y(velocity_pad[2]) - central(interior[1], 2),
            central(interior[0], 2) - central(interior[2], 0),
            central(interior[1], 0) - across_y(velocity_pad[0]),
        ]
    )


def velocity_of(section_two):
    return section_two[1:4] / section_two[0]


def halo_edge_couple(grad_pad, layers):
    return jnp.concatenate([grad_pad[:, :, :layers], grad_pad[:, :, -layers:]], axis=2)


def accumulate_halo_edges(grad_pad, layers, received_halo):
    interior = grad_pad[:, :, layers:-layers]
    interior = interior.at[:, :, :layers].add(received_halo[:, :, :layers])
    return interior.at[:, :, -layers:].add(received_halo[:, :, -layers:])


def body(conserved, target):
    padded_first = padded_2(conserved, (("gy", 2),), 3)
    rate_first, pull_first = jax.vjp(section_rate, padded_first)
    section_one = conserved + DT * rate_first
    padded_second = padded_2(section_one, (("gy", 2),), 3)
    rate_second, pull_second = jax.vjp(section_rate, padded_second)
    section_two = 0.75 * conserved + 0.25 * (section_one + DT * rate_second)
    velocity, pull_velocity = jax.vjp(velocity_of, section_two)
    velocity_pad = padded_2(velocity, (("gy", 2),), 1)
    vorticity, curl_pullback_map = jax.vjp(curl_padded, velocity_pad)
    (padded_velocity_gradient,) = curl_pullback_map(vorticity - target)
    received_halo = padded_2(halo_edge_couple(padded_velocity_gradient, 1), (("gy", 2),), 1)
    velocity_gradient_field = accumulate_halo_edges(padded_velocity_gradient, 1, received_halo)
    (grad_two,) = pull_velocity(velocity_gradient_field)
    (grad_second,) = pull_second(0.25 * DT * grad_two)
    received_halo = padded_2(halo_edge_couple(grad_second, 3), (("gy", 2),), 3)
    grad_one = 0.25 * grad_two + accumulate_halo_edges(grad_second, 3, received_halo)
    (grad_first,) = pull_first(DT * grad_one)
    received_halo = padded_2(halo_edge_couple(grad_first, 3), (("gy", 2),), 3)
    grad_state = 0.75 * grad_two + grad_one + accumulate_halo_edges(grad_first, 3, received_halo)
    return (grad_state, vorticity)


def solution(mesh):
    in_specs = (P(None, "run", "gy", None), P(None, "run", "gy", None))
    out_specs = (P(None, "run", "gy", None), P(None, "run", "gy", None))
    return jax.shard_map(body, mesh=mesh, in_specs=in_specs, out_specs=out_specs, check_vma=False)
```

profile of v0, /device:TPU:0, one launch (start us, length us, event | category | flops | bytes accessed | tf_op | source)
XLA Modules:
  0.0 131.4 jit_solution(15438926129075627048)
XLA Ops:
  0.6 1.0 fusion.138
  2.2 5.1 %collective-permute-start.1 = (f32[5,8,3,128]{3,1,2,0:T(8,128)S(1)}, f32[5,8,3,128]{3,1,2,0:T(8,128)S(1)}, u32[]{:S(2)}, u32[]{:S(2)}) collective-permute-start(f32[5,8,3,128]{3,1,2,0:T(8,128)S(1)} %copy.664), channel_id=1, source_target_pairs={{1,0},{2,1},{3,2},{4,3},{5,4},{6,5},{7,6},{8,7},{9,8},{10,9},{11,1... | collective-permute-start | bytes 184328 | tf_op jit(solution)/shard_map/ppermute | solution.py:20
  7.5 4.7 %while.170 = (s32[]{:T(128)}, f32[5,8,8,128]{3,2,1,0:T(8,128)S(1)}, f32[5,8,8,128]{3,2,1,0:T(8,128)S(1)}, f32[5,8,8,128]{3,2,1,0:T(8,128)S(1)}, s32[]{:T(128)}) while((s32[]{:T(128)}, f32[5,8,8,128]{3,2,1,0:T(8,128)S(1)}, f32[5,8,8,128]{3,2,1,0:T(8,128)S(1)}, f32[5,8,8,128]{3,2,1,0:T(8,128)S(1)}, s32[]{:T(128)}) %tuple.1024), condition=%wide.region_7.8_spmd, body=%wide.region_6.7_spmd.sunk | while | flops 1253378 | bytes 1275461 | solution.py:88
  12.3 1.7 %while.168 = (s32[]{:T(128)}, f32[5,8,8,128]{3,2,1,0:T(8,128)S(1)}, f32[5,8,8,128]{3,2,1,0:T(8,128)S(1)}, f32[5,8,8,128]{3,2,1,0:T(8,128)S(1)}, s32[]{:T(128)}) while((s32[]{:T(128)}, f32[5,8,8,128]{3,2,1,0:T(8,128)S(1)}, f32[5,8,8,128]{3,2,1,0:T(8,128)S(1)}, f32[5,8,8,128]{3,2,1,0:T(8,128)S(1)}, s32[]{:T(128)}) %tuple.1021), condition=%wide.region_2.3_spmd, body=%wide.region_1.2_spmd.sunk | while | flops 1253378 | bytes 1015877 | solution.py:88
  14.7 1.1 while.169
  16.3 4.7 %while.173 = (s32[]{:T(128)}, f32[5,8,8,128]{3,2,1,0:T(8,128)S(1)}, f32[5,8,8,128]{3,2,1,0:T(8,128)S(1)}, f32[5,8,8,128]{3,2,1,0:T(8,128)S(1)}, s32[]{:T(128)}) while((s32[]{:T(128)}, f32[5,8,8,128]{3,2,1,0:T(8,128)S(1)}, f32[5,8,8,128]{3,2,1,0:T(8,128)S(1)}, f32[5,8,8,128]{3,2,1,0:T(8,128)S(1)}, s32[]{:T(128)}) %tuple.1033), condition=%wide.region_15.16_spmd, body=%wide.region_14.15_spmd.sunk | while | flops 1253378 | bytes 1275461 | solution.py:88
  21.1 4.4 %collective-permute-start.3 = (f32[5,8,3,128]{3,1,2,0:T(8,128)S(1)}, f32[5,8,3,128]{3,1,2,0:T(8,128)S(1)}, u32[]{:S(2)}, u32[]{:S(2)}) collective-permute-start(f32[5,8,3,128]{3,1,2,0:T(8,128)S(1)} %copy.624), channel_id=1, source_target_pairs={{1,0},{2,1},{3,2},{4,3},{5,4},{6,5},{7,6},{8,7},{9,8},{10,9},{11,1... | collective-permute-start | bytes 184328 | tf_op jit(solution)/shard_map/ppermute | solution.py:20
  25.6 1.7 %while.171 = (s32[]{:T(128)}, f32[5,8,8,128]{3,2,1,0:T(8,128)S(1)}, f32[5,8,8,128]{3,2,1,0:T(8,128)S(1)}, f32[5,8,8,128]{3,2,1,0:T(8,128)S(1)}, s32[]{:T(128)}) while((s32[]{:T(128)}, f32[5,8,8,128]{3,2,1,0:T(8,128)S(1)}, f32[5,8,8,128]{3,2,1,0:T(8,128)S(1)}, f32[5,8,8,128]{3,2,1,0:T(8,128)S(1)}, s32[]{:T(128)}) %tuple.1030), condition=%wide.region_10.11_spmd, body=%wide.region_9.10_spmd.sunk | while | flops 1253378 | bytes 1015877 | solution.py:88
  28.1 1.1 while.172
  29.8 4.5 %collective-permute-start.5 = (f32[3,8,1,128]{3,1,2,0:T(8,128)S(1)}, f32[3,8,1,128]{3,1,2,0:T(8,128)S(1)}, u32[]{:S(2)}, u32[]{:S(2)}) collective-permute-start(f32[3,8,1,128]{3,1,2,0:T(8,128)S(1)} %bitcast.487), channel_id=1, source_target_pairs={{1,0},{2,1},{3,2},{4,3},{5,4},{6,5},{7,6},{8,7},{9,8},{10,9},{11,1... | collective-permute-start | bytes 36872 | tf_op jit(solution)/shard_map/ppermute | solution.py:20
  34.4 1.3 collective-permute-done.4
  35.8 0.8 copy-done.13
  38.1 4.5 %collective-permute-start.7 = (f32[3,8,1,128]{3,1,2,0:T(8,128)S(1)}, f32[3,8,1,128]{3,1,2,0:T(8,128)S(1)}, u32[]{:S(2)}, u32[]{:S(2)}) collective-permute-start(f32[3,8,1,128]{3,1,2,0:T(8,128)S(1)} %bitcast.484), channel_id=1, source_target_pairs={{1,0},{2,1},{3,2},{4,3},{5,4},{6,5},{7,6},{8,7},{9,8},{10,9},{11,1... | collective-permute-start | bytes 36872 | tf_op jit(solution)/shard_map/ppermute | solution.py:20
  42.6 1.3 collective-permute-done.6
  45.1 5.2 %while.174 = (s32[]{:T(128)}, f32[5,8,14,128]{3,1,2,0:T(8,128)S(1)}, f32[5,8,14,128]{3,1,2,0:T(8,128)S(1)}, f32[5,8,14,128]{3,1,2,0:T(8,128)S(1)}, f32[5,8,14,12...) while((s32[]{:T(128)}, f32[5,8,14,128]{3,1,2,0:T(8,128)S(1)}, ...), condition=%wide.region_19.20_spmd, body=%wide.region_18.19_spmd.sunk | while | flops 5754883 | bytes 5468273 | solution.py:88
  50.4 0.7 fusion.53
  52.0 11.9 %while.176 = (s32[]{:T(128)}, f32[5,8,8,128]{3,2,1,0:T(8,128)S(1)}, f32[5,8,8,128]{3,2,1,0:T(8,128)S(1)}, f32[5,8,8,128]{3,2,1,0:T(8,128)S(1)}, f32[5,8,8,128]{3...) while((s32[]{:T(128)}, f32[5,8,8,128]{3,2,1,0:T(8,128)S(1)}, ...), condition=%wide.region_26.27_spmd, body=%wide.region_25.26_spmd.sunk | while | flops 4251651 | bytes 6389949 | solution.py:88
  53.6 0.7 slice-done
  60.7 0.7 slice-done
  64.6 14.2 %while.175 = (s32[]{:T(128)}, f32[5,8,8,128]{3,2,1,0:T(8,128)S(1)}, f32[5,8,8,128]{3,2,1,0:T(8,128)S(1)}, f32[5,8,8,128]{3,2,1,0:T(8,128)S(1)}, f32[5,8,8,128]{3...) while((s32[]{:T(128)}, f32[5,8,8,128]{3,2,1,0:T(8,128)S(1)}, ...), condition=%wide.region_23.24_spmd, body=%wide.region_22.23_spmd.sunk | while | flops 8732675 | bytes 5177457 | solution.py:88
  78.9 0.7 copy-done.6
  81.2 4.7 %collective-permute-start.9 = (f32[5,8,3,128]{3,1,2,0:T(8,128)S(1)}, f32[5,8,3,128]{3,1,2,0:T(8,128)S(1)}, u32[]{:S(2)}, u32[]{:S(2)}) collective-permute-start(f32[5,8,3,128]{3,1,2,0:T(8,128)S(1)} %copy.650), channel_id=1, source_target_pairs={{1,0},{2,1},{3,2},{4,3},{5,4},{6,5},{7,6},{8,7},{9,8},{10,9},{11,1... | collective-permute-start | bytes 184328 | tf_op jit(solution)/shard_map/ppermute | solution.py:20
  85.9 1.6 %collective-permute-done.8 = f32[5,8,3,128]{3,1,2,0:T(8,128)S(1)} collective-permute-done((f32[5,8,3,128]{3,1,2,0:T(8,128)S(1)}, f32[5,8,3,128]{3,1,2,0:T(8,128)S(1)}, u32[]{:S(2)}, u32[]{:S(2)}) %collective-permute-start.8) | collective-permute-done | bytes 61472 | tf_op jit(solution)/shard_map/ppermute | solution.py:19
  89.0 5.2 %while.177 = (s32[]{:T(128)}, f32[5,8,14,128]{3,1,2,0:T(8,128)S(1)}, f32[5,8,14,128]{3,1,2,0:T(8,128)S(1)}, f32[5,8,14,128]{3,1,2,0:T(8,128)S(1)}, f32[5,8,14,12...) while((s32[]{:T(128)}, f32[5,8,14,128]{3,1,2,0:T(8,128)S(1)}, ...), condition=%wide.region_30.31_spmd, body=%wide.region_29.30_spmd.sunk | while | flops 5754883 | bytes 5468273 | solution.py:88
  96.0 11.9 %while.179 = (s32[]{:T(128)}, f32[5,8,8,128]{3,2,1,0:T(8,128)S(1)}, f32[5,8,8,128]{3,2,1,0:T(8,128)S(1)}, f32[5,8,8,128]{3,2,1,0:T(8,128)S(1)}, f32[5,8,8,128]{3...) while((s32[]{:T(128)}, f32[5,8,8,128]{3,2,1,0:T(8,128)S(1)}, ...), condition=%wide.region_37.38_spmd, body=%wide.region_36.37_spmd.sunk | while | flops 4251651 | bytes 6389949 | solution.py:88
  97.6 0.7 slice-done.2
  100.0 0.7 slice-done.2
  102.3 0.7 slice-done.2
  107.9 14.2 %while.178 = (s32[]{:T(128)}, f32[5,8,8,128]{3,2,1,0:T(8,128)S(1)}, f32[5,8,8,128]{3,2,1,0:T(8,128)S(1)}, f32[5,8,8,128]{3,2,1,0:T(8,128)S(1)}, f32[5,8,8,128]{3...) while((s32[]{:T(128)}, f32[5,8,8,128]{3,2,1,0:T(8,128)S(1)}, ...), condition=%wide.region_34.35_spmd, body=%wide.region_33.34_spmd.sunk | while | flops 8732675 | bytes 5177457 | solution.py:88
  122.3 0.8 copy-done.3
  123.8 4.5 %collective-permute-start.11 = (f32[5,8,3,128]{3,1,2,0:T(8,128)S(1)}, f32[5,8,3,128]{3,1,2,0:T(8,128)S(1)}, u32[]{:S(2)}, u32[]{:S(2)}) collective-permute-start(f32[5,8,3,128]{3,1,2,0:T(8,128)S(1)} %copy.661), channel_id=1, source_target_pairs={{1,0},{2,1},{3,2},{4,3},{5,4},{6,5},{7,6},{8,7},{9,8},{10,9},{11,1... | collective-permute-start | bytes 184328 | tf_op jit(solution)/shard_map/ppermute | solution.py:20
  128.3 1.8 %collective-permute-done.10 = f32[5,8,3,128]{3,1,2,0:T(8,128)S(1)} collective-permute-done((f32[5,8,3,128]{3,1,2,0:T(8,128)S(1)}, f32[5,8,3,128]{3,1,2,0:T(8,128)S(1)}, u32[]{:S(2)}, u32[]{:S(2)}) %collective-permute-start.10) | collective-permute-done | bytes 61472 | tf_op jit(solution)/shard_map/ppermute | solution.py:19
  (1269 shorter events, 82.9 us)
Async XLA Ops:
  1.7 5.6 %copy-start = (f32[5,8,8,128]{3,2,1,0:T(8,128)S(1)}, f32[5,8,8,128]{3,2,1,0:T(8,128)}, u32[]{:S(2)}) copy-start(f32[5,8,8,128]{3,2,1,0:T(8,128)} %param.38) | copy-start | bytes 491524
  1.7 12.4 %collective-permute-start = (f32[5,8,3,128]{3,1,2,0:T(8,128)S(1)}, f32[5,8,3,128]{3,1,2,0:T(8,128)S(1)}, u32[]{:S(2)}, u32[]{:S(2)}) collective-permute-start(f32[5,8,3,128]{3,1,2,0:T(8,128)S(1)} %copy.663), channel_id=1, source_target_pairs={{0,1},{1,2},{2,3},{3,4},{4,5},{5,6},{6,7},{7,8},{8,9},{9,10},{10,1... | collective-permute-start | bytes 184328 | tf_op jit(solution)/shard_map/ppermute | solution.py:19
  2.2 11.9 %collective-permute-start.1 = (f32[5,8,3,128]{3,1,2,0:T(8,128)S(1)}, f32[5,8,3,128]{3,1,2,0:T(8,128)S(1)}, u32[]{:S(2)}, u32[]{:S(2)}) collective-permute-start(f32[5,8,3,128]{3,1,2,0:T(8,128)S(1)} %copy.664), channel_id=1, source_target_pairs={{1,0},{2,1},{3,2},{4,3},{5,4},{6,5},{7,6},{8,7},{9,8},{10,9},{11,1... | collective-permute-start | bytes 184328 | tf_op jit(solution)/shard_map/ppermute | solution.py:20
  21.1 6.4 %collective-permute-start.2 = (f32[5,8,3,128]{3,1,2,0:T(8,128)S(1)}, f32[5,8,3,128]{3,1,2,0:T(8,128)S(1)}, u32[]{:S(2)}, u32[]{:S(2)}) collective-permute-start(f32[5,8,3,128]{3,1,2,0:T(8,128)S(1)} %copy.623), channel_id=1, source_target_pairs={{0,1},{1,2},{2,3},{3,4},{4,5},{5,6},{6,7},{7,8},{8,9},{9,10},{10,1... | collective-permute-start | bytes 184328 | tf_op jit(solution)/shard_map/ppermute | solution.py:19
  21.1 6.3 %collective-permute-start.3 = (f32[5,8,3,128]{3,1,2,0:T(8,128)S(1)}, f32[5,8,3,128]{3,1,2,0:T(8,128)S(1)}, u32[]{:S(2)}, u32[]{:S(2)}) collective-permute-start(f32[5,8,3,128]{3,1,2,0:T(8,128)S(1)} %copy.624), channel_id=1, source_target_pairs={{1,0},{2,1},{3,2},{4,3},{5,4},{6,5},{7,6},{8,7},{9,8},{10,9},{11,1... | collective-permute-start | bytes 184328 | tf_op jit(solution)/shard_map/ppermute | solution.py:20
  29.8 5.8 %collective-permute-start.4 = (f32[3,8,1,128]{3,1,2,0:T(8,128)S(1)}, f32[3,8,1,128]{3,1,2,0:T(8,128)S(1)}, u32[]{:S(2)}, u32[]{:S(2)}) collective-permute-start(f32[3,8,1,128]{3,1,2,0:T(8,128)S(1)} %bitcast.488), channel_id=1, source_target_pairs={{0,1},{1,2},{2,3},{3,4},{4,5},{5,6},{6,7},{7,8},{8,9},{9,10},{10,1... | collective-permute-start | bytes 36872 | tf_op jit(solution)/shard_map/ppermute | solution.py:19
  29.8 5.9 %collective-permute-start.5 = (f32[3,8,1,128]{3,1,2,0:T(8,128)S(1)}, f32[3,8,1,128]{3,1,2,0:T(8,128)S(1)}, u32[]{:S(2)}, u32[]{:S(2)}) collective-permute-start(f32[3,8,1,128]{3,1,2,0:T(8,128)S(1)} %bitcast.487), channel_id=1, source_target_pairs={{1,0},{2,1},{3,2},{4,3},{5,4},{6,5},{7,6},{8,7},{9,8},{10,9},{11,1... | collective-permute-start | bytes 36872 | tf_op jit(solution)/shard_map/ppermute | solution.py:20
  35.7 0.9 copy-start.13
  38.0 5.9 %collective-permute-start.6 = (f32[3,8,1,128]{3,1,2,0:T(8,128)S(1)}, f32[3,8,1,128]{3,1,2,0:T(8,128)S(1)}, u32[]{:S(2)}, u32[]{:S(2)}) collective-permute-start(f32[3,8,1,128]{3,1,2,0:T(8,128)S(1)} %bitcast.486), channel_id=1, source_target_pairs={{0,1},{1,2},{2,3},{3,4},{4,5},{5,6},{6,7},{7,8},{8,9},{9,10},{10,1... | collective-permute-start | bytes 36872 | tf_op jit(solution)/shard_map/ppermute | solution.py:19
  38.1 5.9 %collective-permute-start.7 = (f32[3,8,1,128]{3,1,2,0:T(8,128)S(1)}, f32[3,8,1,128]{3,1,2,0:T(8,128)S(1)}, u32[]{:S(2)}, u32[]{:S(2)}) collective-permute-start(f32[3,8,1,128]{3,1,2,0:T(8,128)S(1)} %bitcast.484), channel_id=1, source_target_pairs={{1,0},{2,1},{3,2},{4,3},{5,4},{6,5},{7,6},{8,7},{9,8},{10,9},{11,1... | collective-permute-start | bytes 36872 | tf_op jit(solution)/shard_map/ppermute | solution.py:20
  53.6 0.7 slice-start
  56.0 0.7 slice-start
  60.7 0.7 slice-start
  78.8 0.8 copy-start.6
  78.8 0.9 copy-start.7
  78.9 0.9 copy-start.8
  78.9 0.9 copy-start.9
  79.9 0.8 copy-start.12
  79.9 0.8 copy-start.10
  80.0 0.8 copy-start.11
  80.0 0.7 copy-start.14
  81.1 6.4 %collective-permute-start.8 = (f32[5,8,3,128]{3,1,2,0:T(8,128)S(1)}, f32[5,8,3,128]{3,1,2,0:T(8,128)S(1)}, u32[]{:S(2)}, u32[]{:S(2)}) collective-permute-start(f32[5,8,3,128]{3,1,2,0:T(8,128)S(1)} %copy.648), channel_id=1, source_target_pairs={{0,1},{1,2},{2,3},{3,4},{4,5},{5,6},{6,7},{7,8},{8,9},{9,10},{10,1... | collective-permute-start | bytes 184328 | tf_op jit(solution)/shard_map/ppermute | solution.py:19
  81.2 6.6 %collective-permute-start.9 = (f32[5,8,3,128]{3,1,2,0:T(8,128)S(1)}, f32[5,8,3,128]{3,1,2,0:T(8,128)S(1)}, u32[]{:S(2)}, u32[]{:S(2)}) collective-permute-start(f32[5,8,3,128]{3,1,2,0:T(8,128)S(1)} %copy.650), channel_id=1, source_target_pairs={{1,0},{2,1},{3,2},{4,3},{5,4},{6,5},{7,6},{8,7},{9,8},{10,9},{11,1... | collective-permute-start | bytes 184328 | tf_op jit(solution)/shard_map/ppermute | solution.py:20
  99.9 0.7 slice-start.2
  102.3 0.7 slice-start.2
  104.7 0.7 slice-start.2
  107.0 0.7 slice-start.2
  122.2 0.8 copy-start.3
  122.2 0.9 copy-start.4
  122.2 0.9 copy-start.5
  123.7 6.4 %collective-permute-start.10 = (f32[5,8,3,128]{3,1,2,0:T(8,128)S(1)}, f32[5,8,3,128]{3,1,2,0:T(8,128)S(1)}, u32[]{:S(2)}, u32[]{:S(2)}) collective-permute-start(f32[5,8,3,128]{3,1,2,0:T(8,128)S(1)} %copy.659), channel_id=1, source_target_pairs={{0,1},{1,2},{2,3},{3,4},{4,5},{5,6},{6,7},{7,8},{8,9},{9,10},{10,1... | collective-permute-start | bytes 184328 | tf_op jit(solution)/shard_map/ppermute | solution.py:19
  123.8 6.6 %collective-permute-start.11 = (f32[5,8,3,128]{3,1,2,0:T(8,128)S(1)}, f32[5,8,3,128]{3,1,2,0:T(8,128)S(1)}, u32[]{:S(2)}, u32[]{:S(2)}) collective-permute-start(f32[5,8,3,128]{3,1,2,0:T(8,128)S(1)} %copy.661), channel_id=1, source_target_pairs={{1,0},{2,1},{3,2},{4,3},{5,4},{6,5},{7,6},{8,7},{9,8},{10,9},{11,1... | collective-permute-start | bytes 184328 | tf_op jit(solution)/shard_map/ppermute | solution.py:20
  (23 other events, 15.5 us)
where the time goes:
time: 132 us; the launch traced here: 131 us
  other arithmetic  47.7 us (36%)
  local copies, waits for them, and re-layouts  41.8 us (32%)
  starting transfers between devices  28.3 us (21%)
  waiting for transfers between devices  6.1 us (5%)
  loops' own time  5.18 us (4%)
  between operations  2.32 us (2%)
    ppermute x6, starting transfers between devices, padded_2(): after = lax.ppermute(first, axis, down)  27.6 us
    add_any x120, other arithmetic, weno_face(): cand_low = (2.0 * far_left - 7.0 * near_left + 11.0 * centre) / 6.0  16 us
    split x260, local copies, waits for them, and re-layouts, offset(): return jnp.roll(values, -shift_by, axis=direction)  13.5 us
    slice x360, local copies, waits for them, and re-layouts, offset(): return jnp.roll(values, -shift_by, axis=direction)  13 us
    dynamic_update_slice x80, other arithmetic, face_values(): return lax.map(jax.checkpoint(single), (plus_part, negative_split_flux))  10.5 us
    ppermute x6, waiting for transfers between devices, padded_2(): before = lax.ppermute(last, axis, up)  6.01 us
    while x20, local copies, waits for them, and re-layouts  6.01 us
    add_any x30, other arithmetic, weno_face(): cand_high = (2.0 * centre + 5.0 * near_right - far_right) / 6.0  5.54 us
  transfers between devices with their start and end apart: 12, of which 5 were waited for; matrix products, arithmetic and copies ran while one was open for 6% of the time, Pallas kernels for 0%

commit v1 on v0

v1 whole, which is shorter than its diff:
```python
import functools

import jax
import jax.numpy as jnp
from jax import lax
from jax.experimental import pallas as pl
from jax.experimental.pallas import tpu as pltpu
from jax.sharding import PartitionSpec as P

SPEED = 2.5
DT = 0.2
X_AXIS, Z_AXIS = 0, 1
MESH = pl.DeviceIdType.MESH


def inv(x):
    return pltpu.reciprocal(x, approx=True)


def prv(x, axis):
    return pltpu.roll(x, 1, axis)


def nxt(x, axis):
    return pltpu.roll(x, x.shape[axis] - 1, axis)


def flow(u):
    ir = inv(u[0])
    v = [u[k] * ir for k in (1, 2, 3)]
    p = 0.4 * (u[4] - 0.5 * (u[1] * v[0] + u[2] * v[1] + u[3] * v[2]))
    return ir, v, p


def split(u, v, p, d):
    vd = v[d]
    flux = [u[d + 1]]
    for k in range(3):
        term = u[k + 1] * vd
        flux.append(term + p if k == d else term)
    flux.append((u[4] + p) * vd)
    out = []
    for f, q in zip(flux, u):
        half, wave = 0.5 * f, (0.5 * SPEED) * q
        out.append((half + wave, half - wave))
    return out


def split_adjoint(u, ir, v, p, d, gp, gm, grad):
    f = [None if a is None else 0.5 * (a + b) for a, b in zip(gp, gm)]
    for k in range(5):
        if gp[k] is not None:
            grad[k] = plus(grad[k], (0.5 * SPEED) * (gp[k] - gm[k]))
    vd = v[d]
    cp = f[d + 1]
    cv = f[1] * u[1] + f[2] * u[2] + f[3] * u[3]
    if f[4] is not None:
        cp = cp + f[4] * vd
        cv = cv + f[4] * (u[4] + p)
        grad[4] = plus(grad[4], f[4] * vd)
    cp = 0.4 * cp
    grad[4] = plus(grad[4], cp)
    cv = cv * ir
    for k in range(3):
        grad[k + 1] = plus(grad[k + 1], f[k + 1] * vd - v[k] * cp)
    grad[d + 1] = grad[d + 1] + (f[0] + cv)
    speed2 = v[0] * v[0] + v[1] * v[1] + v[2] * v[2]
    grad[0] = plus(grad[0], 0.5 * speed2 * cp - cv * vd)


def plus(a, b):
    return b if a is None else a + b


def cell(um, u, up):
    m = up - um
    d = (up - u) - (u - um)
    e = d + d
    q = (13.0 / 3.0) * (d * d) + 0.4
    a, b = m + e, m - e
    return m, d, q + m * m, q + a * a, q + b * b


LINEAR = ((1.0, 3.0), (3.0, 1.0))
SLOPE = ((1.0 / 3.0, 0.5), (0.5, 1.0 / 3.0))


def correction(bm, bc, bp, tm, tp, side):
    lm, lp = LINEAR[side]
    km, kp = SLOPE[side]
    tau = bm - bp
    ym, yc, yp = tau * inv(bm), tau * inv(bc), tau * inv(bp)
    zm, zc, zp = ym * ym, yc * yc, yp * yp
    total = (10.0 + lm * zm) + (6.0 * zc + lp * zp)
    top = (1.0 + zm) * (km * tm) + (1.0 + zp) * (kp * tp)
    return top * inv(total)


def correction_adjoint(h4, bm, bc, bp, tm, tp, side):
    lm, lp = LINEAR[side]
    km, kp = SLOPE[side]
    tau = bm - bp
    rm, rc, rp = inv(bm), inv(bc), inv(bp)
    ym, yc, yp = tau * rm, tau * rc, tau * rp
    zm, zc, zp = ym * ym, yc * yc, yp * yp
    am, ap = 1.0 + zm, 1.0 + zp
    ktm, ktp = km * tm, kp * tp
    rt = inv((10.0 + lm * zm) + (6.0 * zc + lp * zp))
    value = (am * ktm + ap * ktp) * rt
    gs = h4 * rt if side == 0 else -(h4 * rt)
    gv = gs * value
    dm = (gs * ktm - lm * gv) * (ym * rm)
    dc = (-6.0 * gv) * (yc * rc)
    dp = (gs * ktp - lp * gv) * (yp * rp)
    sk = dm + dc + dp
    return sk - dm * ym, -(dc * yc), -(sk + dp * yp), (0.25 * km) * (gs * am), (0.25 * kp) * (gs * ap)


def cell_adjoint(m, d, gc, gr, gl, d_extra, m_extra):
    both = gr + gl
    total = both + gc
    delta = 2.0 * (gr - gl)
    gm = total * m + delta * d + m_extra
    gd = ((13.0 / 3.0) * total + 4.0 * both) * d + delta * m + d_extra
    return gm, gd


def rolled_term(f, axis, side):
    m, d, bc, br, bl = cell(prv(f, axis), f, nxt(f, axis))
    tp = nxt(d, axis) - d
    r = correction(prv(br, axis), bc, nxt(bl, axis), prv(tp, axis), tp, side)
    if side == 0:
        a = (1.0 / 6.0) * d + r
        return a - prv(a, axis) - 0.5 * m
    a = (1.0 / 6.0) * d - r
    return nxt(a, axis) - a - 0.5 * m


def rolled_adjoint(f, lam, h4, axis, side):
    m, d, bc, br, bl = cell(prv(f, axis), f, nxt(f, axis))
    tp = nxt(d, axis) - d
    gbm, gbc, gbp, ctm, ctp = correction_adjoint(
        h4, prv(br, axis), bc, nxt(bl, axis), prv(tp, axis), tp, side
    )
    w = ctp + nxt(ctm, axis)
    extra = (1.0 / 24.0) * h4 + (prv(w, axis) - w)
    gm, gd = cell_adjoint(m, d, gbc, nxt(gbm, axis), prv(gbp, axis), extra, -0.5 * lam)
    return prv(gd + gm, axis) + nxt(gd - gm, axis) - 2.0 * gd


def central(x, axis):
    return 0.5 * (nxt(x, axis) - prv(x, axis))


def kernel(
    rows, c_ref, t_ref, g_ref, o_ref,
    u1, u2, wv, tg, res, rate, two, lam, f1, f2, yc1, yc2, za, gb, pq, gu1, gu2, rg1, rg2,
    send, recv,
):
    size = lax.axis_size("gy")
    me = lax.axis_index("gy")
    right, left = lax.rem(me + 1, size), lax.rem(me + size - 1, size)
    barrier = pltpu.get_barrier_semaphore()
    for other in (left, right):
        pl.semaphore_signal(barrier, inc=1, device_id={"gy": other}, device_id_type=MESH)

    def loop(low, high, body):
        lax.fori_loop(low, high, lambda i, _: (body(i), 0)[1], 0)

    def exchange(slot, pairs):
        copies = []
        for side, (other, (src, dst)) in enumerate(zip((left, right), pairs)):
            copies.append(
                pltpu.make_async_remote_copy(
                    src_ref=src, dst_ref=dst,
                    send_sem=send.at[slot, side], recv_sem=recv.at[slot, side],
                    device_id={"gy": other}, device_id_type=MESH,
                )
            )
        for copy in copies:
            copy.start()
        return copies

    def halo(slot, ref, width):
        return exchange(
            slot,
            (
                (ref.at[:, pl.ds(width, width)], ref.at[:, pl.ds(width + rows, width)]),
                (ref.at[:, pl.ds(rows, width)], ref.at[:, pl.ds(0, width)]),
            ),
        )

    def arrived(copies):
        for copy in copies:
            copy.wait_recv()

    def strided(component, row):
        return pl.ds(component * (8 * rows) + row, 8, stride=rows)

    def load_row(i):
        for c in range(5):
            u1[c, i + 3] = c_ref[strided(c, i), :]
        for c in range(3):
            tg[c, i + 1] = t_ref[strided(c, i), :]

    zero = jnp.zeros((8, 128), jnp.float32)

    loop(0, rows, load_row)
    pl.semaphore_wait(barrier, 2)
    copies_u = halo(0, u1, 3)
    copies_t = halo(1, tg, 1)

    def clear(i):
        for side in range(2):
            for c in range(5):
                for q in range(5):
                    gb[side, c, q, i] = zero
                    gb[side, c, q, i + rows + 3] = zero

    loop(0, 2, clear)

    def clear_pq(i):
        for side in range(2):
            for c in range(5):
                for q in range(3):
                    pq[side, c, q, i] = zero
                    pq[side, c, q, i + rows + 4] = zero

    loop(0, 4, clear_pq)

    def clear_lam(i):
        for c in range(5):
            lam[c, i] = zero
            lam[c, i + rows + 3] = zero

    loop(0, 3, clear_lam)

    def state(ref, row):
        return [ref[c, row] for c in range(5)]

    def flux_y(u_ref, f_ref, row):
        u = state(u_ref, row)
        _, v, p = flow(u)
        for c, pair in enumerate(split(u, v, p, 1)):
            f_ref[0, c, row] = pair[0]
            f_ref[1, c, row] = pair[1]

    def rate_local(u_ref, f_ref):
        def body(i):
            u = state(u_ref, i + 3)
            _, v, p = flow(u)
            for c, pair in enumerate(split(u, v, p, 1)):
                f_ref[0, c, i + 3] = pair[0]
                f_ref[1, c, i + 3] = pair[1]
            fx = split(u, v, p, 0)
            fz = split(u, v, p, 2)
            for c in range(5):
                total = None
                for side in range(2):
                    total = plus(total, rolled_term(fx[c][side], X_AXIS, side))
                    total = plus(total, rolled_term(fz[c][side], Z_AXIS, side))
                rate[c, i] = total

        loop(0, rows, body)

    def rate_y(u_ref, f_ref, yc):
        def edges(i):
            flux_y(u_ref, f_ref, i)
            flux_y(u_ref, f_ref, i + rows + 3)

        loop(0, 3, edges)

        def cells(i):
            for c in range(5):
                for side in range(2):
                    r = i + 1
                    values = cell(f_ref[side, c, r - 1], f_ref[side, c, r], f_ref[side, c, r + 1])
                    for q in range(5):
                        yc[side, c, q, r] = values[q]

        loop(0, rows + 4, cells)

        def faces(k):
            for c in range(5):
                total = None
                for side in range(2):
                    r = k + 2 + side
                    d = yc[side, c, 1, r]
                    x = correction(
                        yc[side, c, 3, r - 1], yc[side, c, 2, r], yc[side, c, 4, r + 1],
                        d - yc[side, c, 1, r - 1], yc[side, c, 1, r + 1] - d, side,
                    )
                    a = (1.0 / 6.0) * d
                    total = plus(total, a + x if side == 0 else a - x)
                za[c, k] = total

        loop(0, rows + 1, faces)

    def whole_rate(yc, c, i):
        return rate[c, i] + (
            (za[c, i + 1] - za[c, i]) - 0.5 * (yc[0, c, 0, i + 3] + yc[1, c, 0, i + 3])
        )

    rate_local(u1, f1)
    arrived(copies_u)
    rate_y(u1, f1, yc1)

    def first(i):
        for c in range(5):
            u2[c, i + 3] = u1[c, i + 3] + DT * whole_rate(yc1, c, i)

    loop(0, rows, first)
    copies_2 = halo(2, u2, 3)

    rate_local(u2, f2)
    arrived(copies_2)
    rate_y(u2, f2, yc2)

    def second(i):
        s = []
        for c in range(4):
            s.append(
                0.75 * u1[c, i + 3] + 0.25 * (u2[c, i + 3] + DT * whole_rate(yc2, c, i))
            )
        ir = inv(s[0])
        two[3, i] = ir
        for k in range(3):
            wv[k, i + 2] = s[k + 1] * ir

    loop(0, rows, second)
    copies_w = halo(3, wv, 2)
    arrived(copies_t)
    arrived(copies_w)

    def curl(i):
        x, y, z = wv[0, i + 1], wv[1, i + 1], wv[2, i + 1]
        vort = (
            0.5 * (wv[2, i + 2] - wv[2, i]) - central(y, Z_AXIS),
            central(x, Z_AXIS) - central(z, X_AXIS),
            central(y, X_AXIS) - 0.5 * (wv[0, i + 2] - wv[0, i]),
        )
        for k in range(3):
            res[k, i] = vort[k] - tg[k, i]
        return vort

    def curl_own(i):
        vort = curl(i + 1)
        for k in range(3):
            o_ref[strided(k, i), :] = vort[k]

    loop(0, rows, curl_own)
    curl(0)
    curl(rows + 1)

    def back_two(i):
        a, b, c = res[0, i + 1], res[1, i + 1], res[2, i + 1]
        gw = (
            0.5 * (res[2, i + 2] - res[2, i]) - central(b, Z_AXIS),
            central(a, Z_AXIS) - central(c, X_AXIS),
            central(b, X_AXIS) - 0.5 * (res[0, i + 2] - res[0, i]),
        )
        ir = two[3, i]
        gw = [ir * g for g in gw]
        grad = [-(gw[0] * wv[0, i + 2] + gw[1] * wv[1, i + 2] + gw[2] * wv[2, i + 2])] + gw
        for c in range(4):
            two[c, i] = grad[c]
            lam[c, i + 3] = (0.25 * DT) * grad[c]

    loop(0, rows, back_two)

    def back_y(slot, u_ref, yc, gu, rg, count):
        def faces(k):
            for c in range(count):
                h4 = 4.0 * (lam[c, k + 2] - lam[c, k + 3])
                for side in range(2):
                    r = k + 2 + side
                    d = yc[side, c, 1, r]
                    gbm, gbc, gbp, ctm, ctp = correction_adjoint(
                        h4, yc[side, c, 3, r - 1], yc[side, c, 2, r], yc[side, c, 4, r + 1],
                        d - yc[side, c, 1, r - 1], yc[side, c, 1, r + 1] - d, side,
                    )
                    centre = (ctm - ctp) + (1.0 / 24.0) * h4
                    for q, value in enumerate((gbm, gbc, gbp, ctm, ctp)):
                        gb[side, c, q, k + 2] = value
                    pq[side, c, 2, r + 1] = centre

        loop(0, rows + 1, faces)

        def cells(j):
            for c in range(count):
                for side in range(2):
                    r = j + 1 + side
                    extra = pq[side, c, 2, r + 1] + (gb[side, c, 4, j] - gb[side, c, 3, j + 2])
                    gm, gd = cell_adjoint(
                        yc[side, c, 0, r], yc[side, c, 1, r],
                        gb[side, c, 1, j + 1], gb[side, c, 0, j + 2], gb[side, c, 2, j],
                        extra, -0.5 * lam[c, r],
                    )
                    pq[side, c, 0, r + 1] = gd + gm
                    pq[side, c, 1, r + 1] = gd - gm

        loop(0, rows + 3, cells)

        def gather(r):
            u = state(u_ref, r)
            ir, v, p = flow(u)
            parts = ([None] * 5, [None] * 5)
            for c in range(count):
                for side in range(2):
                    parts[side][c] = (
                        pq[side, c, 0, r] + pq[side, c, 1, r + 2]
                        - (pq[side, c, 0, r + 1] + pq[side, c, 1, r + 1])
                    )
            grad = [None] * 5
            split_adjoint(u, ir, v, p, 1, parts[0], parts[1], grad)
            for c in range(5):
                gu[c, r] = grad[c]

        loop(0, rows + 6, gather)
        return exchange(
            slot,
            (
                (gu.at[:, pl.ds(0, 3)], rg.at[1]),
                (gu.at[:, pl.ds(rows + 3, 3)], rg.at[0]),
            ),
        )

    def back_local(u_ref, gu, count):
        def body(i):
            u = state(u_ref, i + 3)
            ir, v, p = flow(u)
            grad = [gu[c, i + 3] for c in range(5)]
            for d, axis in ((0, X_AXIS), (2, Z_AXIS)):
                f = split(u, v, p, d)
                parts = ([None] * 5, [None] * 5)
                for c in range(count):
                    value = lam[c, i + 3]
                    h4 = 4.0 * (value - nxt(value, axis))
                    parts[0][c] = rolled_adjoint(f[c][0], value, h4, axis, 0)
                    parts[1][c] = rolled_adjoint(f[c][1], value, prv(h4, axis), axis, 1)
                split_adjoint(u, ir, v, p, d, parts[0], parts[1], grad)
            for c in range(5):
                rate[c, i] = grad[c]

        loop(0, rows, body)

    def add_edges(rg):
        def body(i):
            for c in range(5):
                rate[c, i] = rate[c, i] + rg[0, c, i]

        def body_last(i):
            for c in range(5):
                rate[c, i + rows - 3] = rate[c, i + rows - 3] + rg[1, c, i]

        loop(0, 3, body)
        loop(0, 3, body_last)

    copies_g2 = back_y(4, u2, yc2, gu2, rg2, 4)
    back_local(u2, gu2, 4)
    arrived(copies_g2)
    add_edges(rg2)

    def grad_one(i):
        for c in range(5):
            value = rate[c, i] if c == 4 else 0.25 * two[c, i] + rate[c, i]
            lam[c, i + 3] = DT * value
            two[c, i] = value if c == 4 else 0.75 * two[c, i] + value

    loop(0, rows, grad_one)

    copies_g1 = back_y(5, u1, yc1, gu1, rg1, 5)
    back_local(u1, gu1, 5)
    arrived(copies_g1)
    add_edges(rg1)

    def finish(i):
        for c in range(5):
            g_ref[strided(c, i), :] = two[c, i] + rate[c, i]

    loop(0, rows, finish)
    for copies in (copies_u, copies_t, copies_2, copies_w, copies_g2, copies_g1):
        for copy in copies:
            copy.wait_send()


def body(conserved, target):
    rows = conserved.shape[2]
    tile = conserved.shape[1::2]

    def vmem(*lead):
        return pltpu.VMEM(lead + tile, jnp.float32)

    grad, vorticity = pl.pallas_call(
        functools.partial(kernel, rows),
        out_shape=(
            jax.ShapeDtypeStruct((5 * tile[0] * rows, tile[1]), jnp.float32),
            jax.ShapeDtypeStruct((3 * tile[0] * rows, tile[1]), jnp.float32),
        ),
        in_specs=[pl.BlockSpec(memory_space=pltpu.VMEM)] * 2,
        out_specs=[pl.BlockSpec(memory_space=pltpu.VMEM)] * 2,
        scratch_shapes=[
            vmem(5, rows + 6), vmem(5, rows + 6), vmem(3, rows + 4), vmem(3, rows + 2),
            vmem(3, rows + 2), vmem(5, rows), vmem(5, rows), vmem(5, rows + 6),
            vmem(2, 5, rows + 6), vmem(2, 5, rows + 6),
            vmem(2, 5, 5, rows + 6), vmem(2, 5, 5, rows + 6),
            vmem(5, rows + 1), vmem(2, 5, 5, rows + 5), vmem(2, 5, 3, rows + 8),
            vmem(5, rows + 6), vmem(5, rows + 6), vmem(2, 5, 3), vmem(2, 5, 3),
            pltpu.SemaphoreType.DMA((6, 2)),
            pltpu.SemaphoreType.DMA((6, 2)),
        ],
        compiler_params=pltpu.CompilerParams(
            collective_id=0, has_side_effects=True, vmem_limit_bytes=40 * 1024 * 1024
        ),
    )(conserved.reshape(-1, tile[1]), target.reshape(-1, tile[1]))
    return grad.reshape(conserved.shape), vorticity.reshape(target.shape)


def solution(mesh):
    spec = P(None, "run", "gy", None)
    return jax.shard_map(
        body, mesh=mesh, in_specs=(spec, spec), out_specs=(spec, spec), check_vma=False
    )
```

time: 132 us -> 35.9 us (0.27)
  other arithmetic: 47.7 us -> 0 us
  local copies, waits for them, and re-layouts: 41.8 us -> 3.11 us
  Pallas kernels: 0 us -> 32 us
  starting transfers between devices: 28.3 us -> 0 us
  waiting for transfers between devices: 6.1 us -> 0 us
  loops' own time: 5.18 us -> 0 us
  between operations: 2.32 us -> 0.65 us
    add_any x230 -> x0, other arithmetic: 33.1 us -> none  [the longest x120 16 us: weno_face(): cand_low = (2.0 * far_left - 7.0 * near_left + 11.0 * centre) / 6.0]
    pallas_call x0 -> x1, Pallas kernels: none -> 32 us  [body(): pl.pallas_call(functools.partial(kernel, rows), out_shape=(jax.ShapeDtype...]
    ppermute x12 -> x0, starting transfers between devices: 28.3 us -> none  [the longest x6 27.6 us: padded_2(): after = lax.ppermute(first, axis, down)]
    slice x384 -> x0, local copies, waits for them, and re-layouts: 14.6 us -> none  [the longest x360 13 us: offset(): return jnp.roll(values, -shift_by, axis=direction)]
    split x278 -> x0, local copies, waits for them, and re-layouts: 14.1 us -> none  [the longest x260 13.5 us: offset(): return jnp.roll(values, -shift_by, axis=direction)]
    dynamic_update_slice x80 -> x0, other arithmetic: 10.5 us -> none  [face_values(): return lax.map(jax.checkpoint(single), (plus_part, negative_split_flux))]
    while x32 -> x0, local copies, waits for them, and re-layouts: 6.98 us -> none
    ppermute x12 -> x0, waiting for transfers between devices: 6.1 us -> none  [the longest x6 6.01 us: padded_2(): before = lax.ppermute(last, axis, up)]
  transfers between devices with their start and end apart: 12 -> 0, of which waited for: 5 -> 0; matrix products, arithmetic and copies ran while one was open for 6% -> 0% of each run, Pallas kernels for 0% -> 0%
where the time goes in v1:
time: 35.9 us; the launch traced here: 35.7 us
  Pallas kernels  32 us (89%)
  local copies, waits for them, and re-layouts  3.11 us (9%)
  between operations  0.65 us (2%)
    pallas_call x1, Pallas kernels, body(): pl.pallas_call(functools.partial(kernel, rows), out_shape=(jax.ShapeDtype...  32 us
    unnamed x6, local copies, waits for them, and re-layouts  3.11 us

profile of v1, /device:TPU:0, one launch (start us, length us, event | category | flops | bytes accessed | tf_op | source)
XLA Modules:
  0.0 35.7 jit_solution(15435739543922296053)
XLA Ops:
  0.6 0.0 copy-start
  0.6 0.9 %copy-done = f32[5,8,8,128]{3,2,1,0:T(8,128)S(1)} copy-done((f32[5,8,8,128]{3,2,1,0:T(8,128)S(1)}, f32[5,8,8,128]{3,2,1,0:T(8,128)}, u32[]{:S(2)}) %copy-start) | copy-done | bytes 163864
  1.5 0.0 copy-start.1
  1.5 0.9 %copy-done.1 = f32[3,8,8,128]{3,2,1,0:T(8,128)S(1)} copy-done((f32[3,8,8,128]{3,2,1,0:T(8,128)S(1)}, f32[3,8,8,128]{3,2,1,0:T(8,128)}, u32[]{:S(2)}) %copy-start.1) | copy-done | bytes 98328
  2.4 32.0 %shard_map.41 = (f32[320,128]{1,0:T(8,128)S(1)}, f32[192,128]{1,0:T(8,128)S(1)}) custom-call(f32[320,128]{1,0:T(8,128)S(1)} %bitcast.5, f32[192,128]{1,0:T(8,128)S(1)} %bitcast.7), custom_call_target="tpu_custom_call" | custom-call | tf_op jit(solution)/shard_map/pallas_call | solution.py:494
  34.4 0.7 %copy.6 = f32[5,8,8,128]{3,2,1,0:T(8,128)} copy(f32[5,8,8,128]{3,2,1,0:T(8,128)S(1)} %bitcast.4) | data formatting | bytes 327680
  35.1 0.6 %copy.7 = f32[3,8,8,128]{3,2,1,0:T(8,128)} copy(f32[3,8,8,128]{3,2,1,0:T(8,128)S(1)} %bitcast.6) | data formatting | bytes 196608
Async XLA Ops:
  0.6 0.9 %copy-start = (f32[5,8,8,128]{3,2,1,0:T(8,128)S(1)}, f32[5,8,8,128]{3,2,1,0:T(8,128)}, u32[]{:S(2)}) copy-start(f32[5,8,8,128]{3,2,1,0:T(8,128)} %param.2) | copy-start | bytes 491524
  1.5 0.9 %copy-start.1 = (f32[3,8,8,128]{3,2,1,0:T(8,128)S(1)}, f32[3,8,8,128]{3,2,1,0:T(8,128)}, u32[]{:S(2)}) copy-start(f32[3,8,8,128]{3,2,1,0:T(8,128)} %param.3) | copy-start | bytes 294916

commit v2 on v1

--- a/solution.py
+++ b/solution.py
@@ -89,17 +89,6 @@
     lm, lp = LINEAR[side]
     km, kp = SLOPE[side]
     tau = bm - bp
-    ym, yc, yp = tau * inv(bm), tau * inv(bc), tau * inv(bp)
-    zm, zc, zp = ym * ym, yc * yc, yp * yp
-    total = (10.0 + lm * zm) + (6.0 * zc + lp * zp)
-    top = (1.0 + zm) * (km * tm) + (1.0 + zp) * (kp * tp)
-    return top * inv(total)
-
-
-def correction_adjoint(h4, bm, bc, bp, tm, tp, side):
-    lm, lp = LINEAR[side]
-    km, kp = SLOPE[side]
-    tau = bm - bp
     rm, rc, rp = inv(bm), inv(bc), inv(bp)
     ym, yc, yp = tau * rm, tau * rc, tau * rp
     zm, zc, zp = ym * ym, yc * yc, yp * yp
@@ -107,13 +96,15 @@
     ktm, ktp = km * tm, kp * tp
     rt = inv((10.0 + lm * zm) + (6.0 * zc + lp * zp))
     value = (am * ktm + ap * ktp) * rt
-    gs = h4 * rt if side == 0 else -(h4 * rt)
-    gv = gs * value
-    dm = (gs * ktm - lm * gv) * (ym * rm)
-    dc = (-6.0 * gv) * (yc * rc)
-    dp = (gs * ktp - lp * gv) * (yp * rp)
+    if side == 1:
+        rt = -rt
+    dm = (ktm - lm * value) * (ym * rm)
+    dc = (-6.0 * value) * (yc * rc)
+    dp = (ktp - lp * value) * (yp * rp)
     sk = dm + dc + dp
-    return sk - dm * ym, -(dc * yc), -(sk + dp * yp), (0.25 * km) * (gs * am), (0.25 * kp) * (gs * ap)
+    return value, (
+        rt * (sk - dm * ym), rt * (-dc * yc), rt * (-sk - dp * yp), ((0.25 * km) * rt) * am, ((0.25 * kp) * rt) * ap
+    )
 
 
 def cell_adjoint(m, d, gc, gr, gl, d_extra, m_extra):
@@ -125,10 +116,12 @@
     return gm, gd
 
 
-def rolled_term(f, axis, side):
+def rolled_term(f, axis, side, keep):
     m, d, bc, br, bl = cell(prv(f, axis), f, nxt(f, axis))
     tp = nxt(d, axis) - d
-    r = correction(prv(br, axis), bc, nxt(bl, axis), prv(tp, axis), tp, side)
+    r, coefs = correction(prv(br, axis), bc, nxt(bl, axis), prv(tp, axis), tp, side)
+    if keep is not None:
+        keep((m, d) + coefs)
     if side == 0:
         a = (1.0 / 6.0) * d + r
         return a - prv(a, axis) - 0.5 * m
@@ -136,15 +129,13 @@
     return nxt(a, axis) - a - 0.5 * m
 
 
-def rolled_adjoint(f, lam, h4, axis, side):
-    m, d, bc, br, bl = cell(prv(f, axis), f, nxt(f, axis))
-    tp = nxt(d, axis) - d
-    gbm, gbc, gbp, ctm, ctp = correction_adjoint(
-        h4, prv(br, axis), bc, nxt(bl, axis), prv(tp, axis), tp, side
+def rolled_adjoint(kept, lam, h4, axis):
+    m, d, cbm, cbc, cbp, ctm, ctp = kept
+    w = h4 * ctp + nxt(h4 * ctm, axis)
+    extra = (1.0 / 24.0) * h4 + (prv(w, axis) - w)
+    gm, gd = cell_adjoint(
+        m, d, h4 * cbc, nxt(h4 * cbm, axis), prv(h4 * cbp, axis), extra, -0.5 * lam
     )
-    w = ctp + nxt(ctm, axis)
-    extra = (1.0 / 24.0) * h4 + (prv(w, axis) - w)
-    gm, gd = cell_adjoint(m, d, gbc, nxt(gbm, axis), prv(gbp, axis), extra, -0.5 * lam)
     return prv(gd + gm, axis) + nxt(gd - gm, axis) - 2.0 * gd
 
 
@@ -153,10 +144,16 @@
 
 
 def kernel(
-    rows, c_ref, t_ref, g_ref, o_ref,
-    u1, u2, wv, tg, res, rate, two, lam, f1, f2, yc1, yc2, za, gb, pq, gu1, gu2, rg1, rg2,
-    send, recv,
+    rows, c_any, t_any, g_ref, o_ref,
+    c_ref, t_ref, u1, u2, wv, tg, res, rate, two, ivs, lam, f1, f2, yc1, yc2, za, ys1, ys2,
+    st1, st2, pq, gu1, gu2, rg1, rg2, local, send, recv,
 ):
+    loads = [
+        pltpu.make_async_copy(c_any, c_ref, local.at[0]),
+        pltpu.make_async_copy(t_any, t_ref, local.at[1]),
+    ]
+    for load in loads:
+        load.start()
     size = lax.axis_size("gy")
     me = lax.axis_index("gy")
     right, left = lax.rem(me + 1, size), lax.rem(me + size - 1, size)
@@ -205,6 +202,8 @@
 
     zero = jnp.zeros((8, 128), jnp.float32)
 
+    for load in loads:
+        load.wait()
     loop(0, rows, load_row)
     pl.semaphore_wait(barrier, 2)
     copies_u = halo(0, u1, 3)
@@ -214,19 +213,19 @@
         for side in range(2):
             for c in range(5):
                 for q in range(5):
-                    gb[side, c, q, i] = zero
-                    gb[side, c, q, i + rows + 3] = zero
+                    ys1[side, c, q, i] = zero
+                    ys1[side, c, q, i + rows + 3] = zero
 
     loop(0, 2, clear)
 
     def clear_pq(i):
         for side in range(2):
             for c in range(5):
-                for q in range(3):
+                for q in range(2):
                     pq[side, c, q, i] = zero
-                    pq[side, c, q, i + rows + 4] = zero
-
-    loop(0, 4, clear_pq)
+                    pq[side, c, q, i + rows + 5] = zero
+
+    loop(0, 3, clear_pq)
 
     def clear_lam(i):
         for c in range(5):
@@ -245,30 +244,36 @@
             f_ref[0, c, row] = pair[0]
             f_ref[1, c, row] = pair[1]
 
-    def rate_local(u_ref, f_ref):
-        def body(i):
-            u = state(u_ref, i + 3)
-            _, v, p = flow(u)
+    def row_rate(u_ref, f_ref, st, pad, count, i):
+        u = state(u_ref, i + pad)
+        _, v, p = flow(u)
+        if st is not None:
             for c, pair in enumerate(split(u, v, p, 1)):
-                f_ref[0, c, i + 3] = pair[0]
-                f_ref[1, c, i + 3] = pair[1]
-            fx = split(u, v, p, 0)
-            fz = split(u, v, p, 2)
-            for c in range(5):
-                total = None
-                for side in range(2):
-                    total = plus(total, rolled_term(fx[c][side], X_AXIS, side))
-                    total = plus(total, rolled_term(fz[c][side], Z_AXIS, side))
-                rate[c, i] = total
-
-        loop(0, rows, body)
-
-    def rate_y(u_ref, f_ref, yc):
+                f_ref[0, c, i + pad] = pair[0]
+                f_ref[1, c, i + pad] = pair[1]
+        fx = split(u, v, p, 0)
+        fz = split(u, v, p, 2)
+        for c in range(5):
+            total = None
+            for side in range(2):
+                for number, f, axis in ((0, fx, X_AXIS), (1, fz, Z_AXIS)):
+
+                    def keep(values):
+                        for q, value in enumerate(values):
+                            st[number, side, c, q, i] = value
+
+                    use = keep if st is not None and c < count else None
+                    total = plus(total, rolled_term(f[c][side], axis, side, use))
+            rate[c, i + pad - 3] = total
+
+    def rate_y(u_ref, f_ref, yc, ys, pad, count):
+        extra = pad - 3
+
         def edges(i):
             flux_y(u_ref, f_ref, i)
-            flux_y(u_ref, f_ref, i + rows + 3)
-
-        loop(0, 3, edges)
+            flux_y(u_ref, f_ref, i + rows + pad)
+
+        loop(0, pad, edges)
 
         def cells(i):
             for c in range(5):
@@ -278,7 +283,7 @@
                     for q in range(5):
                         yc[side, c, q, r] = values[q]
 
-        loop(0, rows + 4, cells)
+        loop(0, rows + 2 * pad - 2, cells)
 
         def faces(k):
             for c in range(5):
@@ -286,51 +291,58 @@
                 for side in range(2):
                     r = k + 2 + side
                     d = yc[side, c, 1, r]
-                    x = correction(
+                    x, coefs = correction(
                         yc[side, c, 3, r - 1], yc[side, c, 2, r], yc[side, c, 4, r + 1],
                         d - yc[side, c, 1, r - 1], yc[side, c, 1, r + 1] - d, side,
                     )
+                    if c < count:
+                        for q, value in enumerate(coefs):
+                            ys[side, c, q, k + 2 - extra] = value
                     a = (1.0 / 6.0) * d
                     total = plus(total, a + x if side == 0 else a - x)
                 za[c, k] = total
 
-        loop(0, rows + 1, faces)
+        loop(0, rows + 1 + 2 * extra, faces)
 
     def whole_rate(yc, c, i):
         return rate[c, i] + (
             (za[c, i + 1] - za[c, i]) - 0.5 * (yc[0, c, 0, i + 3] + yc[1, c, 0, i + 3])
         )
 
-    rate_local(u1, f1)
+    loop(0, rows, lambda i: row_rate(u1, f1, st1, 3, 5, i))
     arrived(copies_u)
-    rate_y(u1, f1, yc1)
+    rate_y(u1, f1, yc1, ys1, 3, 5)
 
     def first(i):
         for c in range(5):
-            u2[c, i + 3] = u1[c, i + 3] + DT * whole_rate(yc1, c, i)
+            u2[c, i + 5] = u1[c, i + 3] + DT * whole_rate(yc1, c, i)
 
     loop(0, rows, first)
-    copies_2 = halo(2, u2, 3)
-
-    rate_local(u2, f2)
+    copies_2 = halo(2, u2, 5)
+
+    loop(0, rows, lambda i: row_rate(u2, f2, st2, 5, 4, i))
     arrived(copies_2)
-    rate_y(u2, f2, yc2)
+
+    def beside(i):
+        row_rate(u2, f2, None, 5, 4, i - 2)
+        row_rate(u2, f2, None, 5, 4, i + rows)
+
+    loop(0, 2, beside)
+    rate_y(u2, f2, yc2, ys2, 5, 4)
 
     def second(i):
         s = []
         for c in range(4):
             s.append(
-                0.75 * u1[c, i + 3] + 0.25 * (u2[c, i + 3] + DT * whole_rate(yc2, c, i))
+                0.75 * u1[c, i + 1] + 0.25 * (u2[c, i + 3] + DT * whole_rate(yc2, c, i))
             )
         ir = inv(s[0])
-        two[3, i] = ir
+        ivs[i] = ir
         for k in range(3):
-            wv[k, i + 2] = s[k + 1] * ir
-
-    loop(0, rows, second)
-    copies_w = halo(3, wv, 2)
+            wv[k, i] = s[k + 1] * ir
+
+    loop(0, rows + 4, second)
     arrived(copies_t)
-    arrived(copies_w)
 
     def curl(i):
         x, y, z = wv[0, i + 1], wv[1, i + 1], wv[2, i + 1]
@@ -359,7 +371,7 @@
             central(a, Z_AXIS) - central(c, X_AXIS),
             central(b, X_AXIS) - 0.5 * (res[0, i + 2] - res[0, i]),
         )
-        ir = two[3, i]
+        ir = ivs[i + 2]
         gw = [ir * g for g in gw]
         grad = [-(gw[0] * wv[0, i + 2] + gw[1] * wv[1, i + 2] + gw[2] * wv[2, i + 2])] + gw
         for c in range(4):
@@ -368,33 +380,24 @@
 
     loop(0, rows, back_two)
 
-    def back_y(slot, u_ref, yc, gu, rg, count):
-        def faces(k):
-            for c in range(count):
-                h4 = 4.0 * (lam[c, k + 2] - lam[c, k + 3])
-                for side in range(2):
-                    r = k + 2 + side
-                    d = yc[side, c, 1, r]
-                    gbm, gbc, gbp, ctm, ctp = correction_adjoint(
-                        h4, yc[side, c, 3, r - 1], yc[side, c, 2, r], yc[side, c, 4, r + 1],
-                        d - yc[side, c, 1, r - 1], yc[side, c, 1, r + 1] - d, side,
-                    )
-                    centre = (ctm - ctp) + (1.0 / 24.0) * h4
-                    for q, value in enumerate((gbm, gbc, gbp, ctm, ctp)):
-                        gb[side, c, q, k + 2] = value
-                    pq[side, c, 2, r + 1] = centre
-
-        loop(0, rows + 1, faces)
+    def back_y(slot, u_ref, yc, ys, gu, rg, pad, count):
+        extra = pad - 3
 
         def cells(j):
             for c in range(count):
+                l0, l1, l2, l3 = (lam[c, j + n] for n in range(4))
+                before, here, after = 4.0 * (l0 - l1), 4.0 * (l1 - l2), 4.0 * (l2 - l3)
                 for side in range(2):
                     r = j + 1 + side
-                    extra = pq[side, c, 2, r + 1] + (gb[side, c, 4, j] - gb[side, c, 3, j + 2])
+                    tm, tp = here * ys[side, c, 3, j + 1], here * ys[side, c, 4, j + 1]
+                    slope = (tm - tp) + (
+                        before * ys[side, c, 4, j] - after * ys[side, c, 3, j + 2]
+                    )
                     gm, gd = cell_adjoint(
-                        yc[side, c, 0, r], yc[side, c, 1, r],
-                        gb[side, c, 1, j + 1], gb[side, c, 0, j + 2], gb[side, c, 2, j],
-                        extra, -0.5 * lam[c, r],
+                        yc[side, c, 0, r + extra], yc[side, c, 1, r + extra],
+                        here * ys[side, c, 1, j + 1], after * ys[side, c, 0, j + 2],
+                        before * ys[side, c, 2, j],
+                        slope + (1.0 / 24.0) * here, -0.5 * (l2 if side else l1),
                     )
                     pq[side, c, 0, r + 1] = gd + gm
                     pq[side, c, 1, r + 1] = gd - gm
@@ -402,7 +405,7 @@
         loop(0, rows + 3, cells)
 
         def gather(r):
-            u = state(u_ref, r)
+            u = state(u_ref, r + extra)
             ir, v, p = flow(u)
             parts = ([None] * 5, [None] * 5)
             for c in range(count):
@@ -416,28 +419,34 @@
             for c in range(5):
                 gu[c, r] = grad[c]
 
-        loop(0, rows + 6, gather)
-        return exchange(
+        def gather_edges(r):
+            gather(r)
+            gather(r + rows + 3)
+
+        loop(0, 3, gather_edges)
+        copies = exchange(
             slot,
             (
                 (gu.at[:, pl.ds(0, 3)], rg.at[1]),
                 (gu.at[:, pl.ds(rows + 3, 3)], rg.at[0]),
             ),
         )
-
-    def back_local(u_ref, gu, count):
+        loop(3, rows + 3, gather)
+        return copies
+
+    def back_local(u_ref, gu, st, pad, count):
         def body(i):
-            u = state(u_ref, i + 3)
+            u = state(u_ref, i + pad)
             ir, v, p = flow(u)
             grad = [gu[c, i + 3] for c in range(5)]
-            for d, axis in ((0, X_AXIS), (2, Z_AXIS)):
-                f = split(u, v, p, d)
+            for number, d, axis in ((0, 0, X_AXIS), (1, 2, Z_AXIS)):
                 parts = ([None] * 5, [None] * 5)
                 for c in range(count):
                     value = lam[c, i + 3]
                     h4 = 4.0 * (value - nxt(value, axis))
-                    parts[0][c] = rolled_adjoint(f[c][0], value, h4, axis, 0)
-                    parts[1][c] = rolled_adjoint(f[c][1], value, prv(h4, axis), axis, 1)
+                    for side, h in enumerate((h4, prv(h4, axis))):
+                        kept = [st[number, side, c, q, i] for q in range(7)]
+                        parts[side][c] = rolled_adjoint(kept, value, h, axis)
                 split_adjoint(u, ir, v, p, d, parts[0], parts[1], grad)
             for c in range(5):
                 rate[c, i] = grad[c]
@@ -456,8 +465,8 @@
         loop(0, 3, body)
         loop(0, 3, body_last)
 
-    copies_g2 = back_y(4, u2, yc2, gu2, rg2, 4)
-    back_local(u2, gu2, 4)
+    copies_g2 = back_y(3, u2, yc2, ys2, gu2, rg2, 5, 4)
+    back_local(u2, gu2, st2, 5, 4)
     arrived(copies_g2)
     add_edges(rg2)
 
@@ -469,8 +478,8 @@
 
     loop(0, rows, grad_one)
 
-    copies_g1 = back_y(5, u1, yc1, gu1, rg1, 5)
-    back_local(u1, gu1, 5)
+    copies_g1 = back_y(4, u1, yc1, ys1, gu1, rg1, 3, 5)
+    back_local(u1, gu1, st1, 3, 5)
     arrived(copies_g1)
     add_edges(rg1)
 
@@ -479,7 +488,7 @@
             g_ref[strided(c, i), :] = two[c, i] + rate[c, i]
 
     loop(0, rows, finish)
-    for copies in (copies_u, copies_t, copies_2, copies_w, copies_g2, copies_g1):
+    for copies in (copies_u, copies_t, copies_2, copies_g2, copies_g1):
         for copy in copies:
             copy.wait_send()
 
@@ -497,17 +506,21 @@
             jax.ShapeDtypeStruct((5 * tile[0] * rows, tile[1]), jnp.float32),
             jax.ShapeDtypeStruct((3 * tile[0] * rows, tile[1]), jnp.float32),
         ),
-        in_specs=[pl.BlockSpec(memory_space=pltpu.VMEM)] * 2,
+        in_specs=[pl.BlockSpec(memory_space=pltpu.HBM)] * 2,
         out_specs=[pl.BlockSpec(memory_space=pltpu.VMEM)] * 2,
         scratch_shapes=[
-            vmem(5, rows + 6), vmem(5, rows + 6), vmem(3, rows + 4), vmem(3, rows + 2),
-            vmem(3, rows + 2), vmem(5, rows), vmem(5, rows), vmem(5, rows + 6),
-            vmem(2, 5, rows + 6), vmem(2, 5, rows + 6),
-            vmem(2, 5, 5, rows + 6), vmem(2, 5, 5, rows + 6),
-            vmem(5, rows + 1), vmem(2, 5, 5, rows + 5), vmem(2, 5, 3, rows + 8),
+            pltpu.VMEM((5 * tile[0] * rows, tile[1]), jnp.float32),
+            pltpu.VMEM((3 * tile[0] * rows, tile[1]), jnp.float32),
+            vmem(5, rows + 6), vmem(5, rows + 10), vmem(3, rows + 4), vmem(3, rows + 2),
+            vmem(3, rows + 2), vmem(5, rows + 4), vmem(5, rows), vmem(rows + 4), vmem(5, rows + 6),
+            vmem(2, 5, rows + 6), vmem(2, 5, rows + 10),
+            vmem(2, 5, 5, rows + 6), vmem(2, 5, 5, rows + 10),
+            vmem(5, rows + 5), vmem(2, 5, 5, rows + 5), vmem(2, 4, 5, rows + 5),
+            vmem(2, 2, 5, 7, rows), vmem(2, 2, 4, 7, rows), vmem(2, 5, 2, rows + 8),
             vmem(5, rows + 6), vmem(5, rows + 6), vmem(2, 5, 3), vmem(2, 5, 3),
-            pltpu.SemaphoreType.DMA((6, 2)),
-            pltpu.SemaphoreType.DMA((6, 2)),
+            pltpu.SemaphoreType.DMA((2,)),
+            pltpu.SemaphoreType.DMA((5, 2)),
+            pltpu.SemaphoreType.DMA((5, 2)),
         ],
         compiler_params=pltpu.CompilerParams(
             collective_id=0, has_side_effects=True, vmem_limit_bytes=40 * 1024 * 1024

time: 35.9 us -> 33.9 us (0.944)
  Pallas kernels: 32 us -> 29.9 us
    pallas_call x1, Pallas kernels: 32 us -> 29.9 us  [body(): pl.pallas_call(functools.partial(kernel, rows), out_shape=(jax.ShapeDtype...]
where the time goes in v2:
time: 33.9 us; the launch traced here: 33.7 us
  Pallas kernels  29.9 us (88%)
  local copies, waits for them, and re-layouts  3.11 us (9%)
  between operations  0.65 us (2%)
    pallas_call x1, Pallas kernels, body(): pl.pallas_call(functools.partial(kernel, rows), out_shape=(jax.ShapeDtype...  29.9 us
    unnamed x6, local copies, waits for them, and re-layouts  3.11 us

profile of v2, /device:TPU:0, one launch (start us, length us, event | category | flops | bytes accessed | tf_op | source)
XLA Modules:
  0.0 33.7 jit_solution(15294965426407402703)
XLA Ops:
  0.6 0.0 copy-start
  0.6 0.9 %copy-done = f32[5,8,8,128]{3,2,1,0:T(8,128)S(1)} copy-done((f32[5,8,8,128]{3,2,1,0:T(8,128)S(1)}, f32[5,8,8,128]{3,2,1,0:T(8,128)}, u32[]{:S(2)}) %copy-start) | copy-done | bytes 163864
  1.5 0.0 copy-start.1
  1.5 0.9 %copy-done.1 = f32[3,8,8,128]{3,2,1,0:T(8,128)S(1)} copy-done((f32[3,8,8,128]{3,2,1,0:T(8,128)S(1)}, f32[3,8,8,128]{3,2,1,0:T(8,128)}, u32[]{:S(2)}) %copy-start.1) | copy-done | bytes 98328
  2.4 29.9 %shard_map.41 = (f32[320,128]{1,0:T(8,128)S(1)}, f32[192,128]{1,0:T(8,128)S(1)}) custom-call(f32[320,128]{1,0:T(8,128)S(1)} %bitcast.5, f32[192,128]{1,0:T(8,128)S(1)} %bitcast.7), custom_call_target="tpu_custom_call" | custom-call | tf_op jit(solution)/shard_map/pallas_call | solution.py:503
  32.4 0.7 %copy.6 = f32[5,8,8,128]{3,2,1,0:T(8,128)} copy(f32[5,8,8,128]{3,2,1,0:T(8,128)S(1)} %bitcast.4) | data formatting | bytes 327680
  33.1 0.6 %copy.7 = f32[3,8,8,128]{3,2,1,0:T(8,128)} copy(f32[3,8,8,128]{3,2,1,0:T(8,128)S(1)} %bitcast.6) | data formatting | bytes 196608
Async XLA Ops:
  0.6 0.9 %copy-start = (f32[5,8,8,128]{3,2,1,0:T(8,128)S(1)}, f32[5,8,8,128]{3,2,1,0:T(8,128)}, u32[]{:S(2)}) copy-start(f32[5,8,8,128]{3,2,1,0:T(8,128)} %param.2) | copy-start | bytes 491524
  1.5 0.9 %copy-start.1 = (f32[3,8,8,128]{3,2,1,0:T(8,128)S(1)}, f32[3,8,8,128]{3,2,1,0:T(8,128)}, u32[]{:S(2)}) copy-start(f32[3,8,8,128]{3,2,1,0:T(8,128)} %param.3) | copy-start | bytes 294916

commit v3 on v2

--- a/solution.py
+++ b/solution.py
@@ -96,21 +96,19 @@
     ktm, ktp = km * tm, kp * tp
     rt = inv((10.0 + lm * zm) + (6.0 * zc + lp * zp))
     value = (am * ktm + ap * ktp) * rt
-    if side == 1:
-        rt = -rt
     dm = (ktm - lm * value) * (ym * rm)
     dc = (-6.0 * value) * (yc * rc)
     dp = (ktp - lp * value) * (yp * rp)
     sk = dm + dc + dp
     return value, (
-        rt * (sk - dm * ym), rt * (-dc * yc), rt * (-sk - dp * yp), ((0.25 * km) * rt) * am, ((0.25 * kp) * rt) * ap
+        sk - dm * ym, dc * yc, sk + dp * yp, (0.25 * km) * am, (0.25 * kp) * ap, rt if side == 0 else -rt
     )
 
 
 def cell_adjoint(m, d, gc, gr, gl, d_extra, m_extra):
-    both = gr + gl
-    total = both + gc
-    delta = 2.0 * (gr - gl)
+    both = gr - gl
+    total = both - gc
+    delta = 2.0 * (gr + gl)
     gm = total * m + delta * d + m_extra
     gd = ((13.0 / 3.0) * total + 4.0 * both) * d + delta * m + d_extra
     return gm, gd
@@ -130,11 +128,12 @@
 
 
 def rolled_adjoint(kept, lam, h4, axis):
-    m, d, cbm, cbc, cbp, ctm, ctp = kept
-    w = h4 * ctp + nxt(h4 * ctm, axis)
+    m, d, cbm, cbc, cbp, ctm, ctp, factor = kept
+    hs = h4 * factor
+    w = hs * ctp + nxt(hs * ctm, axis)
     extra = (1.0 / 24.0) * h4 + (prv(w, axis) - w)
     gm, gd = cell_adjoint(
-        m, d, h4 * cbc, nxt(h4 * cbm, axis), prv(h4 * cbp, axis), extra, -0.5 * lam
+        m, d, hs * cbc, nxt(hs * cbm, axis), prv(hs * cbp, axis), extra, -0.5 * lam
     )
     return prv(gd + gm, axis) + nxt(gd - gm, axis) - 2.0 * gd
 
@@ -164,6 +163,10 @@
     def loop(low, high, body):
         lax.fori_loop(low, high, lambda i, _: (body(i), 0)[1], 0)
 
+    def each_row(body):
+        step = 2 if rows % 2 == 0 else 1
+        loop(0, rows // step, lambda i: [body(step * i + n) for n in range(step)])
+
     def exchange(slot, pairs):
         copies = []
         for side, (other, (src, dst)) in enumerate(zip((left, right), pairs)):
@@ -212,7 +215,7 @@
     def clear(i):
         for side in range(2):
             for c in range(5):
-                for q in range(5):
+                for q in range(6):
                     ys1[side, c, q, i] = zero
                     ys1[side, c, q, i + rows + 3] = zero
 
@@ -253,7 +256,7 @@
                 f_ref[1, c, i + pad] = pair[1]
         fx = split(u, v, p, 0)
         fz = split(u, v, p, 2)
-        for c in range(5):
+        for c in range(count):
             total = None
             for side in range(2):
                 for number, f, axis in ((0, fx, X_AXIS), (1, fz, Z_AXIS)):
@@ -262,7 +265,7 @@
                         for q, value in enumerate(values):
                             st[number, side, c, q, i] = value
 
-                    use = keep if st is not None and c < count else None
+                    use = keep if st is not None else None
                     total = plus(total, rolled_term(f[c][side], axis, side, use))
             rate[c, i + pad - 3] = total
 
@@ -276,7 +279,7 @@
         loop(0, pad, edges)
 
         def cells(i):
-            for c in range(5):
+            for c in range(count):
                 for side in range(2):
                     r = i + 1
                     values = cell(f_ref[side, c, r - 1], f_ref[side, c, r], f_ref[side, c, r + 1])
@@ -286,7 +289,7 @@
         loop(0, rows + 2 * pad - 2, cells)
 
         def faces(k):
-            for c in range(5):
+            for c in range(count):
                 total = None
                 for side in range(2):
                     r = k + 2 + side
@@ -295,9 +298,8 @@
                         yc[side, c, 3, r - 1], yc[side, c, 2, r], yc[side, c, 4, r + 1],
                         d - yc[side, c, 1, r - 1], yc[side, c, 1, r + 1] - d, side,
                     )
-                    if c < count:
-                        for q, value in enumerate(coefs):
-                            ys[side, c, q, k + 2 - extra] = value
+                    for q, value in enumerate(coefs):
+                        ys[side, c, q, k + 2 - extra] = value
                     a = (1.0 / 6.0) * d
                     total = plus(total, a + x if side == 0 else a - x)
                 za[c, k] = total
@@ -309,7 +311,7 @@
             (za[c, i + 1] - za[c, i]) - 0.5 * (yc[0, c, 0, i + 3] + yc[1, c, 0, i + 3])
         )
 
-    loop(0, rows, lambda i: row_rate(u1, f1, st1, 3, 5, i))
+    each_row(lambda i: row_rate(u1, f1, st1, 3, 5, i))
     arrived(copies_u)
     rate_y(u1, f1, yc1, ys1, 3, 5)
 
@@ -320,7 +322,7 @@
     loop(0, rows, first)
     copies_2 = halo(2, u2, 5)
 
-    loop(0, rows, lambda i: row_rate(u2, f2, st2, 5, 4, i))
+    each_row(lambda i: row_rate(u2, f2, st2, 5, 4, i))
     arrived(copies_2)
 
     def beside(i):
@@ -389,14 +391,16 @@
                 before, here, after = 4.0 * (l0 - l1), 4.0 * (l1 - l2), 4.0 * (l2 - l3)
                 for side in range(2):
                     r = j + 1 + side
-                    tm, tp = here * ys[side, c, 3, j + 1], here * ys[side, c, 4, j + 1]
-                    slope = (tm - tp) + (
-                        before * ys[side, c, 4, j] - after * ys[side, c, 3, j + 2]
+                    b, h, a = (
+                        x * ys[side, c, 5, j + n] for n, x in enumerate((before, here, after))
+                    )
+                    slope = h * (ys[side, c, 3, j + 1] - ys[side, c, 4, j + 1]) + (
+                        b * ys[side, c, 4, j] - a * ys[side, c, 3, j + 2]
                     )
                     gm, gd = cell_adjoint(
                         yc[side, c, 0, r + extra], yc[side, c, 1, r + extra],
-                        here * ys[side, c, 1, j + 1], after * ys[side, c, 0, j + 2],
-                        before * ys[side, c, 2, j],
+                        h * ys[side, c, 1, j + 1], a * ys[side, c, 0, j + 2],
+                        b * ys[side, c, 2, j],
                         slope + (1.0 / 24.0) * here, -0.5 * (l2 if side else l1),
                     )
                     pq[side, c, 0, r + 1] = gd + gm
@@ -445,13 +449,13 @@
                     value = lam[c, i + 3]
                     h4 = 4.0 * (value - nxt(value, axis))
                     for side, h in enumerate((h4, prv(h4, axis))):
-                        kept = [st[number, side, c, q, i] for q in range(7)]
+                        kept = [st[number, side, c, q, i] for q in range(8)]
                         parts[side][c] = rolled_adjoint(kept, value, h, axis)
                 split_adjoint(u, ir, v, p, d, parts[0], parts[1], grad)
             for c in range(5):
                 rate[c, i] = grad[c]
 
-        loop(0, rows, body)
+        each_row(body)
 
     def add_edges(rg):
         def body(i):
@@ -515,8 +519,8 @@
             vmem(3, rows + 2), vmem(5, rows + 4), vmem(5, rows), vmem(rows + 4), vmem(5, rows + 6),
             vmem(2, 5, rows + 6), vmem(2, 5, rows + 10),
             vmem(2, 5, 5, rows + 6), vmem(2, 5, 5, rows + 10),
-            vmem(5, rows + 5), vmem(2, 5, 5, rows + 5), vmem(2, 4, 5, rows + 5),
-            vmem(2, 2, 5, 7, rows), vmem(2, 2, 4, 7, rows), vmem(2, 5, 2, rows + 8),
+            vmem(5, rows + 5), vmem(2, 5, 6, rows + 5), vmem(2, 4, 6, rows + 5),
+            vmem(2, 2, 5, 8, rows), vmem(2, 2, 4, 8, rows), vmem(2, 5, 2, rows + 8),
             vmem(5, rows + 6), vmem(5, rows + 6), vmem(2, 5, 3), vmem(2, 5, 3),
             pltpu.SemaphoreType.DMA((2,)),
             pltpu.SemaphoreType.DMA((5, 2)),

time: 33.9 us -> 33.2 us (0.979)
  Pallas kernels: 29.9 us -> 29.2 us
    pallas_call x1, Pallas kernels: 29.9 us -> 29.2 us  [body(): pl.pallas_call(functools.partial(kernel, rows), out_shape=(jax.ShapeDtype...]
where the time goes in v3:
time: 33.2 us; the launch traced here: 33 us
  Pallas kernels  29.2 us (88%)
  local copies, waits for them, and re-layouts  3.11 us (9%)
  between operations  0.65 us (2%)
    pallas_call x1, Pallas kernels, body(): pl.pallas_call(functools.partial(kernel, rows), out_shape=(jax.ShapeDtype...  29.2 us
    unnamed x6, local copies, waits for them, and re-layouts  3.11 us

profile of v3, /device:TPU:0, one launch (start us, length us, event | category | flops | bytes accessed | tf_op | source)
XLA Modules:
  0.0 33.0 jit_solution(10289975514501418107)
XLA Ops:
  0.6 0.0 copy-start
  0.6 0.9 %copy-done = f32[5,8,8,128]{3,2,1,0:T(8,128)S(1)} copy-done((f32[5,8,8,128]{3,2,1,0:T(8,128)S(1)}, f32[5,8,8,128]{3,2,1,0:T(8,128)}, u32[]{:S(2)}) %copy-start) | copy-done | bytes 163864
  1.5 0.0 copy-start.1
  1.5 0.9 %copy-done.1 = f32[3,8,8,128]{3,2,1,0:T(8,128)S(1)} copy-done((f32[3,8,8,128]{3,2,1,0:T(8,128)S(1)}, f32[3,8,8,128]{3,2,1,0:T(8,128)}, u32[]{:S(2)}) %copy-start.1) | copy-done | bytes 98328
  2.4 29.2 %shard_map.41 = (f32[320,128]{1,0:T(8,128)S(1)}, f32[192,128]{1,0:T(8,128)S(1)}) custom-call(f32[320,128]{1,0:T(8,128)S(1)} %bitcast.5, f32[192,128]{1,0:T(8,128)S(1)} %bitcast.7), custom_call_target="tpu_custom_call" | custom-call | tf_op jit(solution)/shard_map/pallas_call | solution.py:507
  31.7 0.7 %copy.6 = f32[5,8,8,128]{3,2,1,0:T(8,128)} copy(f32[5,8,8,128]{3,2,1,0:T(8,128)S(1)} %bitcast.4) | data formatting | bytes 327680
  32.3 0.6 %copy.7 = f32[3,8,8,128]{3,2,1,0:T(8,128)} copy(f32[3,8,8,128]{3,2,1,0:T(8,128)S(1)} %bitcast.6) | data formatting | bytes 196608
Async XLA Ops:
  0.6 0.9 %copy-start = (f32[5,8,8,128]{3,2,1,0:T(8,128)S(1)}, f32[5,8,8,128]{3,2,1,0:T(8,128)}, u32[]{:S(2)}) copy-start(f32[5,8,8,128]{3,2,1,0:T(8,128)} %param.2) | copy-start | bytes 491524
  1.5 0.9 %copy-start.1 = (f32[3,8,8,128]{3,2,1,0:T(8,128)S(1)}, f32[3,8,8,128]{3,2,1,0:T(8,128)}, u32[]{:S(2)}) copy-start(f32[3,8,8,128]{3,2,1,0:T(8,128)} %param.3) | copy-start | bytes 294916

commit v4 on v3

--- a/solution.py
+++ b/solution.py
@@ -143,16 +143,10 @@
 
 
 def kernel(
-    rows, c_any, t_any, g_ref, o_ref,
-    c_ref, t_ref, u1, u2, wv, tg, res, rate, two, ivs, lam, f1, f2, yc1, yc2, za, ys1, ys2,
-    st1, st2, pq, gu1, gu2, rg1, rg2, local, send, recv,
+    rows, c_ref, t_ref, g_ref, o_ref,
+    u1, u2, wv, tg, res, rate, two, ivs, lam, f1, f2, yc1, yc2, za, ys1, ys2,
+    st1, st2, pq, gu1, gu2, rg1, rg2, send, recv,
 ):
-    loads = [
-        pltpu.make_async_copy(c_any, c_ref, local.at[0]),
-        pltpu.make_async_copy(t_any, t_ref, local.at[1]),
-    ]
-    for load in loads:
-        load.start()
     size = lax.axis_size("gy")
     me = lax.axis_index("gy")
     right, left = lax.rem(me + 1, size), lax.rem(me + size - 1, size)
@@ -205,8 +199,6 @@
 
     zero = jnp.zeros((8, 128), jnp.float32)
 
-    for load in loads:
-        load.wait()
     loop(0, rows, load_row)
     pl.semaphore_wait(barrier, 2)
     copies_u = halo(0, u1, 3)
@@ -406,7 +398,11 @@
                     pq[side, c, 0, r + 1] = gd + gm
                     pq[side, c, 1, r + 1] = gd - gm
 
-        loop(0, rows + 3, cells)
+        def cells_edges(j):
+            cells(j)
+            cells(j + rows)
+
+        loop(0, 3, cells_edges)
 
         def gather(r):
             u = state(u_ref, r + extra)
@@ -435,6 +431,7 @@
                 (gu.at[:, pl.ds(rows + 3, 3)], rg.at[0]),
             ),
         )
+        loop(3, rows, cells)
         loop(3, rows + 3, gather)
         return copies
 
@@ -510,11 +507,9 @@
             jax.ShapeDtypeStruct((5 * tile[0] * rows, tile[1]), jnp.float32),
             jax.ShapeDtypeStruct((3 * tile[0] * rows, tile[1]), jnp.float32),
         ),
-        in_specs=[pl.BlockSpec(memory_space=pltpu.HBM)] * 2,
+        in_specs=[pl.BlockSpec(memory_space=pltpu.VMEM)] * 2,
         out_specs=[pl.BlockSpec(memory_space=pltpu.VMEM)] * 2,
         scratch_shapes=[
-            pltpu.VMEM((5 * tile[0] * rows, tile[1]), jnp.float32),
-            pltpu.VMEM((3 * tile[0] * rows, tile[1]), jnp.float32),
             vmem(5, rows + 6), vmem(5, rows + 10), vmem(3, rows + 4), vmem(3, rows + 2),
             vmem(3, rows + 2), vmem(5, rows + 4), vmem(5, rows), vmem(rows + 4), vmem(5, rows + 6),
             vmem(2, 5, rows + 6), vmem(2, 5, rows + 10),
@@ -522,7 +517,6 @@
             vmem(5, rows + 5), vmem(2, 5, 6, rows + 5), vmem(2, 4, 6, rows + 5),
             vmem(2, 2, 5, 8, rows), vmem(2, 2, 4, 8, rows), vmem(2, 5, 2, rows + 8),
             vmem(5, rows + 6), vmem(5, rows + 6), vmem(2, 5, 3), vmem(2, 5, 3),
-            pltpu.SemaphoreType.DMA((2,)),
             pltpu.SemaphoreType.DMA((5, 2)),
             pltpu.SemaphoreType.DMA((5, 2)),
         ],

time: 33.2 us -> 32.3 us (0.973)
  Pallas kernels: 29.2 us -> 28.3 us
    pallas_call x1, Pallas kernels: 29.2 us -> 28.3 us  [body(): pl.pallas_call(functools.partial(kernel, rows), out_shape=(jax.ShapeDtype...]
where the time goes in v4:
time: 32.3 us; the launch traced here: 32.1 us
  Pallas kernels  28.3 us (88%)
  local copies, waits for them, and re-layouts  3.11 us (10%)
  between operations  0.65 us (2%)
    pallas_call x1, Pallas kernels, body(): pl.pallas_call(functools.partial(kernel, rows), out_shape=(jax.ShapeDtype...  28.3 us
    unnamed x6, local copies, waits for them, and re-layouts  3.11 us

profile of v4, /device:TPU:0, one launch (start us, length us, event | category | flops | bytes accessed | tf_op | source)
XLA Modules:
  0.0 32.1 jit_solution(2136643684113456890)
XLA Ops:
  0.6 0.0 copy-start
  0.6 0.9 %copy-done = f32[5,8,8,128]{3,2,1,0:T(8,128)S(1)} copy-done((f32[5,8,8,128]{3,2,1,0:T(8,128)S(1)}, f32[5,8,8,128]{3,2,1,0:T(8,128)}, u32[]{:S(2)}) %copy-start) | copy-done | bytes 163864
  1.5 0.0 copy-start.1
  1.5 0.9 %copy-done.1 = f32[3,8,8,128]{3,2,1,0:T(8,128)S(1)} copy-done((f32[3,8,8,128]{3,2,1,0:T(8,128)S(1)}, f32[3,8,8,128]{3,2,1,0:T(8,128)}, u32[]{:S(2)}) %copy-start.1) | copy-done | bytes 98328
  2.4 28.3 %shard_map.41 = (f32[320,128]{1,0:T(8,128)S(1)}, f32[192,128]{1,0:T(8,128)S(1)}) custom-call(f32[320,128]{1,0:T(8,128)S(1)} %bitcast.5, f32[192,128]{1,0:T(8,128)S(1)} %bitcast.7), custom_call_target="tpu_custom_call" | custom-call | tf_op jit(solution)/shard_map/pallas_call | solution.py:504
  30.8 0.7 %copy.6 = f32[5,8,8,128]{3,2,1,0:T(8,128)} copy(f32[5,8,8,128]{3,2,1,0:T(8,128)S(1)} %bitcast.4) | data formatting | bytes 327680
  31.5 0.6 %copy.7 = f32[3,8,8,128]{3,2,1,0:T(8,128)} copy(f32[3,8,8,128]{3,2,1,0:T(8,128)S(1)} %bitcast.6) | data formatting | bytes 196608
Async XLA Ops:
  0.6 0.9 %copy-start = (f32[5,8,8,128]{3,2,1,0:T(8,128)S(1)}, f32[5,8,8,128]{3,2,1,0:T(8,128)}, u32[]{:S(2)}) copy-start(f32[5,8,8,128]{3,2,1,0:T(8,128)} %param.2) | copy-start | bytes 491524
  1.5 0.9 %copy-start.1 = (f32[3,8,8,128]{3,2,1,0:T(8,128)S(1)}, f32[3,8,8,128]{3,2,1,0:T(8,128)}, u32[]{:S(2)}) copy-start(f32[3,8,8,128]{3,2,1,0:T(8,128)} %param.3) | copy-start | bytes 294916
